TPU v7x, 32 devices: a whole 2x2x4 slice. The times are simulated.
32 devices in a mesh: group: 2 (over y), ens: 4 (over z), row: 2 (over x), col: 2 (over core).
Axes of the slice: x: 2, y: 2, z: 4, core: 2. Of those that a mesh axis runs over, the one named last changes fastest.
Arguments:
- fields: bfloat16 [4, 128, 256, 128], P('ens', ('group', 'row'), 'col'), parts along dimension 1, may hold values from -6 to 6
- conv_weight: bfloat16 [7, 7, 128], replicated, may hold values from -0.875 to 0.875
- conv_gain: bfloat16 [128], replicated, may hold values from 0.099609375 to 1.8984375
- mlp_in: bfloat16 [128, 512], replicated, may hold values from -0.5 to 0.5
- mlp_out: bfloat16 [512, 128], replicated, may hold values from -0.25 to 0.25
- layer_scale: bfloat16 [128], replicated, may hold values from 0.099609375 to 1.8984375
- attn_gain: bfloat16 [128], replicated, may hold values from 0.099609375 to 1.8984375
- qkv_weight: bfloat16 [3, 128, 128], replicated, may hold values from -1 to 1
- out_weight: bfloat16 [128, 128], replicated, may hold values from -0.5 to 0.5
Outputs:
- result: bfloat16 [4, 128, 256, 128], P('ens', ('group', 'row'), 'col'), parts along dimension 1
There are 2 independent parts, one for each index of `group`. A program takes and returns all parts, laid end to end along the dimension named above; an argument that names none is the same for every part. Nothing has to cross between parts.
All inputs are finite; a program needn't handle non-finite values.
Results may differ from a plain program's by a relative error of at most 0.0065.
Values may be sent and summed in bfloat16 or wider, within the bound.
A program may use at most 64 MiB of HBM per device.

v0:
```python
import jax
import jax.numpy as jnp
from jax import lax
from jax.sharding import PartitionSpec as P

HEADS = 4
KERNEL = 7


def extended(array, sides, width):
    for axis, dim in sides:
        devices, length = (lax.axis_size(axis), array.shape[dim])
        up = [(i, (i + 1) % devices) for i in range(devices - 1)]
        down = [(j, i) for i, j in up]
        last = lax.slice_in_dim(array, length - width, length, axis=dim)
        first = lax.slice_in_dim(array, 0, width, axis=dim)
        before = lax.ppermute(last, axis, up)
        after = lax.ppermute(first, axis, down)
        array = jnp.concatenate([before, array, after], axis=dim)
    return array


def layer_norm(values, gain_vec):
    center = values - jnp.mean(values, axis=-1, keepdims=True)
    spread = jnp.mean(center * center, axis=-1, keepdims=True)
    return center * lax.rsqrt(spread + 1e-06) * gain_vec.astype(jnp.float32)


def mix_members(flat_rows, attn_gain, qkv_weight):
    count, pixels, width = flat_rows.shape
    head_dim = width // HEADS
    normed = layer_norm(flat_rows.astype(jnp.float32), attn_gain).astype(jnp.bfloat16)
    project = jnp.einsum(
        "mpc,jcd->jmpd", normed, qkv_weight, preferred_element_type=jnp.float32
    ).astype(jnp.bfloat16)
    split = project.reshape(3, count, pixels, HEADS, head_dim)
    scores = jnp.einsum(
        "mphd,nphd->hmnp", split[0], split[1], preferred_element_type=jnp.float32
    ) * head_dim ** (-0.5)
    top = jnp.max(scores, axis=2, keepdims=True)
    expo = jnp.exp(scores - top)
    weights = (expo / jnp.sum(expo, axis=2, keepdims=True)).astype(jnp.bfloat16)
    mixed = jnp.einsum(
        "hmnp,nphd->mphd", weights, split[2], preferred_element_type=jnp.float32
    ).astype(jnp.bfloat16)
    return mixed.reshape(count, pixels, width)


def shards(
    fields, conv_weight, conv_gain, mlp_in, mlp_out, layer_scale, attn_gain, qkv_weight, out_weight
):
    members, rows, cols, width = fields.shape
    padded = extended(fields, (("row", 1), ("col", 2)), 3)
    taps = conv_weight.astype(jnp.float32)
    total = jnp.zeros((members, rows, cols, width), jnp.float32)
    for row_tap in range(KERNEL):
        band = padded[:, row_tap : row_tap + rows, :, :]
        partial_row = band[:, :, 0:cols, :].astype(jnp.float32) * taps[row_tap, 0]
        for col_tap in range(1, KERNEL):
            partial_row = (
                partial_row
                + band[:, :, col_tap : col_tap + cols, :].astype(jnp.float32)
                * taps[row_tap, col_tap]
            )
        total = total + partial_row
    normed = layer_norm(total, conv_gain).astype(jnp.bfloat16).reshape(members * rows * cols, width)
    inner = jax.nn.gelu(
        jnp.dot(normed, mlp_in, preferred_element_type=jnp.float32), approximate=True
    ).astype(jnp.bfloat16)
    branch = jnp.dot(inner, mlp_out, preferred_element_type=jnp.float32).reshape(
        members, rows, cols, width
    )
    middle = (fields.astype(jnp.float32) + layer_scale.astype(jnp.float32) * branch).astype(
        jnp.bfloat16
    )
    block = lax.all_to_all(middle, "ens", split_axis=1, concat_axis=0, tiled=True)
    count, block_rows, block_cols, block_width = block.shape
    flat_rows = block.reshape(count, block_rows * block_cols, block_width)
    mixed = mix_members(flat_rows, attn_gain, qkv_weight)
    projected = jnp.einsum("mpc,cd->mpd", mixed, out_weight, preferred_element_type=jnp.float32)
    outcome = (flat_rows.astype(jnp.float32) + projected).astype(jnp.bfloat16)
    outcome = outcome.reshape(count, block_rows, block_cols, block_width)
    gathered = outcome
    gathered = lax.all_to_all(gathered, "ens", split_axis=0, concat_axis=1, tiled=True)
    return gathered


def solution(mesh):
    return jax.shard_map(
        shards,
        mesh=mesh,
        in_specs=(P("ens", ("group", "row"), "col", None), P(), P(), P(), P(), P(), P(), P(), P()),
        out_specs=P("ens", ("group", "row"), "col", None),
        check_vma=False,
    )
```

profile of v0, /device:TPU:0, one launch (start us, length us, event | category | flops | bytes accessed | tf_op | source)
XLA Modules:
  0.0 169.5 jit_solution(12458972681998692937)
XLA Ops:
  0.0 0.0 copy-start
  0.0 0.0 copy-start.1
  0.0 1.0 fusion.44
  1.1 4.8 %collective-permute-start = (bf16[1,3,128,128]{3,2,0,1:T(8,128)(2,1)S(1)}, bf16[1,3,128,128]{3,2,0,1:T(8,128)(2,1)S(1)}, u32[]{:S(2)}, u32[]{:S(2)}) collective-permute-start(bf16[1,3,128,128]{3,2,0,1:T(8,128)(2,1)S(1)} %get-tuple-element.14), channel_id=1, source_target_pairs={{0,2},{1,3},{4,6},{5,7},{8,10},{9,11},{12,14},{13,15},{16,18},{17,... | collective-permute-start | bytes 294920 | tf_op jit(solution)/shard_map/ppermute | solution.py:17
  5.9 1.3 collective-permute-start.1
  7.2 0.7 convert_element_type.209
  8.0 0.1 collective-permute-done
  8.1 4.3 %collective-permute-done.1 = bf16[1,3,128,128]{3,2,0,1:T(8,128)(2,1)S(1)} collective-permute-done((bf16[1,3,128,128]{3,2,0,1:T(8,128)(2,1)S(1)}, bf16[1,3,128,128]{3,2,0,1:T(8,128)(2,1)S(1)}, u32[]{:S(2)}, u32[]{:S(2)}) %collective-permute-start.1) | collective-permute-done | bytes 98336 | tf_op jit(solution)/shard_map/ppermute | solution.py:18
  12.4 0.9 pad_maximum_fusion.5
  13.3 1.3 collective-permute-start.2
  14.6 1.3 collective-permute-start.3
  16.0 0.7 convert_element_type.257
  16.6 0.7 convert_element_type.207
  17.3 0.0 collective-permute-done.2
  17.3 0.5 collective-permute-done.3
  17.7 0.0 copy-done.1
  17.7 1.8 %maximum_maximum_fusion = (bf16[1,38,131,128]{3,2,0,1:T(8,128)(2,1)S(1)}, bf16[1,38,131,128]{3,2,0,1:T(8,128)(2,1)S(1)}) fusion(bf16[1,3,128,128]{3,2,0,1:T(8,128)(2,1)S(1)} %collective-permute-done.1, bf16[1,32,128,128]{3,2,0,1:T(8,128)(2,1)S(1)} %bitcast.150, bf16[1,3,128,128]{3,2,0,1:T(8,128)(2,1)S(1)} %collective-permute-done, ...), kind=kLoop, calls=%fused_computation.34 | loop fusion | flops 10194944 | bytes 3852288 | tf_op jit(solution)/shard_map/concatenate | solution.py:19
  19.5 18.9 %fusion.41 = (f32[32,128]{1,0:T(8,128)S(1)}, f32[1,32,128,128]{3,2,0,1:T(8,128)S(1)}) fusion(f32[128]{0:T(128)S(1)} %get-tuple-element.17, bf16[1,38,131,128]{3,2,0,1:T(8,128)(2,1)S(1)} %get-tuple-element.11, f32[128]{0:T(128)S(1)} %get-tuple-element.18, f32[128]{0:T(128)S(1)} %get-tuple-element.19, f32[128]{0:T(128)S(1)} %get-tuple-element.20, ...), kind=kLoop, calls=%fused_computation.121 | loop fusion | flops 80211968 | bytes 47424000 | tf_op jit(solution)/shard_map/reduce_sum | solution.py:24
  38.5 1.3 multiply_reduce_fusion.1
  39.8 0.0 copy-start.5
  39.8 1.2 multiply_convert_fusion.1
  41.1 0.0 copy-done
  41.1 0.0 copy-done.5
  41.1 0.0 copy-start.2
  41.1 4.4 %fusion.19 = f32[4096,128]{1,0:T(8,128)} fusion(bf16[512,128]{1,0:T(8,128)(2,1)S(1)} %copy-done, bf16[4096,128]{1,0:T(8,128)(2,1)S(1)} %bitcast.159, bf16[128,512]{1,0:T(8,128)(2,1)S(1)} %copy-done.5), kind=kOutput, calls=%fused_computation.29 | convolution fusion | flops 1092616192 | bytes 3407872 | tf_op jit(solution)/shard_map/dot_general | solution.py:70
  45.5 0.0 copy-done.2
  45.5 2.9 %fusion.18 = bf16[1,32,128,128]{3,2,0,1:T(8,128)(2,1)} fusion(f32[1,32,128,128]{3,2,0,1:T(8,128)} %bitcast.158, f32[128]{0:T(128)S(1)} %convert_element_type.207, bf16[1,32,128,128]{3,2,1,0:T(8,128)(2,1)S(1)} %copy-done.2), kind=kLoop, calls=%fused_computation.23 | loop fusion | flops 2097152 | bytes 4194816 | tf_op jit(solution)/shard_map/convert_element_type | solution.py:73
  48.4 0.0 copy-start.6
  48.4 0.0 copy-start.3
  48.4 5.0 %all-to-all-start = ((bf16[1,32,128,128]{3,2,0,1:T(8,128)(2,1)}), bf16[1,32,128,128]{3,2,0,1:T(8,128)(2,1)S(1)}, u32[]{:S(2)}, u32[]{:S(2)}) async-start(bf16[1,32,128,128]{3,2,0,1:T(8,128)(2,1)} %fusion.18), calls=%async_computation | async-start | bytes 2097152 | tf_op jit(solution)/shard_map/all_to_all | solution.py:76
  53.4 0.0 copy-done.6
  53.4 26.6 %all-to-all-done = bf16[1,32,128,128]{3,2,0,1:T(8,128)(2,1)S(1)} async-done(((bf16[1,32,128,128]{3,2,0,1:T(8,128)(2,1)}), bf16[1,32,128,128]{3,2,0,1:T(8,128)(2,1)S(1)}, u32[]{:S(2)}, u32[]{:S(2)}) %all-to-all-start) | async-done | bytes 1048608 | tf_op jit(solution)/shard_map/all_to_all | solution.py:76
  80.0 0.3 convert_reduce_fusion
  80.4 1.3 multiply_reduce_fusion
  81.8 0.0 copy-done.3
  81.8 2.1 %convert_bitcast_fusion = bf16[3,4,1024,128]{2,3,0,1:T(8,128)(2,1)S(1)} fusion(f32[128]{0:T(128)S(1)} %convert_element_type.264, f32[4,1024]{1,0:T(4,128)S(1)} %rsqrt.21, f32[4,1024]{1,0:T(4,128)S(1)} %div.25, bf16[3,128,128]{2,1,0:T(8,128)(2,1)S(1)} %copy-done.3, bf16[4,1024,128]{2,1,0:T(8,128)(2,1)S(1)} %bitcast.146), kind=kOutput, calls=%fused_computation.12 | convolution fusion | flops 406847488 | bytes 4325888 | tf_op jit(solution)/shard_map/mpc,jcd->jmpd/dot_general | solution.py:33
  83.8 1.7 fusion.43
  85.5 6.8 %copy.44 = bf16[4,1024,4,32]{3,0,1,2:T(4,128)(2,1)} copy(bf16[4,1024,4,32]{1,3,2,0:T(8,128)(2,1)} %bitcast.156) | data formatting | bytes 2097152 | tf_op jit(solution)/shard_map/squeeze | solution.py:38
  92.3 6.8 %copy.45 = bf16[4,1024,4,32]{3,0,1,2:T(4,128)(2,1)} copy(bf16[4,1024,4,32]{1,3,2,0:T(8,128)(2,1)} %bitcast.155) | data formatting | bytes 2097152 | tf_op jit(solution)/shard_map/squeeze | solution.py:38
  99.1 8.8 %fusion.47 = f32[4,1024,4,4]{3,2,1,0:T(4,128)} fusion(bf16[4,1024,4,32]{3,0,1,2:T(4,128)(2,1)} %copy.44, bf16[4,1024,4,32]{3,0,1,2:T(4,128)(2,1)} %copy.45), kind=kOutput, calls=%fused_computation.126 | convolution fusion | flops 4194304 | bytes 2359296 | tf_op jit(solution)/shard_map/mphd,nphd->hmnp/dot_general | solution.py:37
  107.9 6.8 %copy.46 = f32[4,1024,4,4]{1,2,3,0:T(4,128)S(1)} copy(f32[4,1024,4,4]{3,2,1,0:T(4,128)} %fusion.47) | data formatting | bytes 524288 | tf_op jit(solution)/shard_map/mphd,nphd->hmnp/dot_general | solution.py:37
  114.7 0.4 fusion.45
  115.1 0.1 divide_convert_fusion
  115.2 5.5 %copy.48 = bf16[4,4,4,1024]{2,1,0,3:T(4,128)(2,1)} copy(bf16[4,4,4,1024]{3,2,1,0:T(4,128)(2,1)S(1)} %divide_convert_fusion) | data formatting | bytes 262144 | tf_op jit(solution)/shard_map/convert_element_type | solution.py:42
  120.6 5.3 %copy.47 = bf16[4,1024,4,32]{3,0,2,1:T(4,128)(2,1)} copy(bf16[4,1024,4,32]{1,3,2,0:T(8,128)(2,1)S(1)} %bitcast.154) | data formatting | bytes 2097152 | tf_op jit(solution)/shard_map/squeeze | solution.py:44
  126.0 8.3 %fusion.9 = bf16[4,1024,4,32]{3,0,2,1:T(4,128)(2,1)} fusion(bf16[4,1024,4,32]{3,0,2,1:T(4,128)(2,1)} %copy.47, bf16[4,4,4,1024]{2,1,0,3:T(4,128)(2,1)} %copy.48), kind=kOutput, calls=%fused_computation.11 | convolution fusion | flops 4718592 | bytes 2228224 | tf_op jit(solution)/shard_map/hmnp,nphd->mphd/dot_general | solution.py:43
  134.3 0.0 copy-start.4
  134.3 5.5 %copy.49 = bf16[4,1024,4,32]{1,3,2,0:T(8,128)(2,1)S(1)} copy(bf16[4,1024,4,32]{3,0,2,1:T(4,128)(2,1)} %fusion.9) | data formatting | bytes 2097152 | tf_op jit(solution)/shard_map/convert_element_type | solution.py:45
  139.9 0.0 copy-done.4
  139.9 0.5 add_convert_fusion
  140.3 28.2 %all_to_all.21 = bf16[4,8,128,128]{3,2,1,0:T(8,128)(2,1)S(1)} all-to-all(bf16[4,8,128,128]{3,2,1,0:T(8,128)(2,1)S(1)} %bitcast.153), channel_id=1, replica_groups=mesh['group'=2,'ens'=4,'row'=2,'col'=2] {'ens'}, dimensions={0} | all-to-all | bytes 2097152 | tf_op jit(solution)/shard_map/all_to_all | solution.py:84
  168.6 1.0 copy.56
  (10 shorter events, 0.1 us)
Async XLA Ops:
  0.0 41.1 %copy-start = (bf16[512,128]{1,0:T(8,128)(2,1)S(1)}, bf16[512,128]{1,0:T(8,128)(2,1)}, u32[]{:S(2)}) copy-start(bf16[512,128]{1,0:T(8,128)(2,1)} %param.13) | copy-start | bytes 393220
  0.0 17.7 %copy-start.1 = (bf16[1,32,128,128]{3,2,1,0:T(8,128)(2,1)S(1)}, bf16[1,32,128,128]{3,2,1,0:T(8,128)(2,1)}, u32[]{:S(2)}) copy-start(bf16[1,32,128,128]{3,2,1,0:T(8,128)(2,1)} %param.9) | copy-start | bytes 3145732
  1.1 7.0 %collective-permute-start = (bf16[1,3,128,128]{3,2,0,1:T(8,128)(2,1)S(1)}, bf16[1,3,128,128]{3,2,0,1:T(8,128)(2,1)S(1)}, u32[]{:S(2)}, u32[]{:S(2)}) collective-permute-start(bf16[1,3,128,128]{3,2,0,1:T(8,128)(2,1)S(1)} %get-tuple-element.14), channel_id=1, source_target_pairs={{0,2},{1,3},{4,6},{5,7},{8,10},{9,11},{12,14},{13,15},{16,18},{17,... | collective-permute-start | bytes 294920 | tf_op jit(solution)/shard_map/ppermute | solution.py:17
  5.9 6.5 %collective-permute-start.1 = (bf16[1,3,128,128]{3,2,0,1:T(8,128)(2,1)S(1)}, bf16[1,3,128,128]{3,2,0,1:T(8,128)(2,1)S(1)}, u32[]{:S(2)}, u32[]{:S(2)}) collective-permute-start(bf16[1,3,128,128]{3,2,0,1:T(8,128)(2,1)S(1)} %get-tuple-element.15), channel_id=1, source_target_pairs={{2,0},{3,1},{6,4},{7,5},{10,8},{11,9},{14,12},{15,13},{18,16},{19,... | collective-permute-start | bytes 294920 | tf_op jit(solution)/shard_map/ppermute | solution.py:18
  13.3 3.9 %collective-permute-start.2 = (bf16[1,38,3,128]{3,2,0,1:T(4,128)(2,1)S(1)}, bf16[1,38,3,128]{3,2,0,1:T(4,128)(2,1)S(1)}, u32[]{:S(2)}, u32[]{:S(2)}) collective-permute-start(bf16[1,38,3,128]{3,2,0,1:T(4,128)(2,1)S(1)} %get-tuple-element.12), channel_id=1, source_target_pairs={{0,1},{2,3},{4,5},{6,7},{8,9},{10,11},{12,13},{14,15},{16,17},{18,... | collective-permute-start | bytes 87560 | tf_op jit(solution)/shard_map/ppermute | solution.py:17
  14.6 3.1 %collective-permute-start.3 = (bf16[1,38,3,128]{3,2,0,1:T(4,128)(2,1)S(1)}, bf16[1,38,3,128]{3,2,0,1:T(4,128)(2,1)S(1)}, u32[]{:S(2)}, u32[]{:S(2)}) collective-permute-start(bf16[1,38,3,128]{3,2,0,1:T(4,128)(2,1)S(1)} %get-tuple-element.13), channel_id=1, source_target_pairs={{1,0},{3,2},{5,4},{7,6},{9,8},{11,10},{13,12},{15,14},{17,16},{19,... | collective-permute-start | bytes 87560 | tf_op jit(solution)/shard_map/ppermute | solution.py:18
  39.8 1.3 copy-start.5
  41.1 4.5 %copy-start.2 = (bf16[1,32,128,128]{3,2,1,0:T(8,128)(2,1)S(1)}, bf16[1,32,128,128]{3,2,1,0:T(8,128)(2,1)}, u32[]{:S(2)}) copy-start(bf16[1,32,128,128]{3,2,1,0:T(8,128)(2,1)} %param.9) | copy-start | bytes 3145732
  48.4 5.0 %copy-start.6 = (bf16[128]{0:T(256)(128)(2,1)S(1)}, bf16[128]{0:T(256)(128)(2,1)}, u32[]{:S(2)}) copy-start(bf16[128]{0:T(256)(128)(2,1)} %param.15) | copy-start | bytes 772
  48.4 33.3 %copy-start.3 = (bf16[3,128,128]{2,1,0:T(8,128)(2,1)S(1)}, bf16[3,128,128]{2,1,0:T(8,128)(2,1)}, u32[]{:S(2)}) copy-start(bf16[3,128,128]{2,1,0:T(8,128)(2,1)} %param.16) | copy-start | bytes 294916
  48.4 31.6 %all-to-all-start = ((bf16[1,32,128,128]{3,2,0,1:T(8,128)(2,1)}), bf16[1,32,128,128]{3,2,0,1:T(8,128)(2,1)S(1)}, u32[]{:S(2)}, u32[]{:S(2)}) async-start(bf16[1,32,128,128]{3,2,0,1:T(8,128)(2,1)} %fusion.18), calls=%async_computation | async-start | bytes 2097152 | tf_op jit(solution)/shard_map/all_to_all | solution.py:76
  134.3 5.5 %copy-start.4 = (bf16[128,128]{1,0:T(8,128)(2,1)S(1)}, bf16[128,128]{1,0:T(8,128)(2,1)}, u32[]{:S(2)}) copy-start(bf16[128,128]{1,0:T(8,128)(2,1)} %param.17) | copy-start | bytes 98308
where the time goes:
time: 171 us; the launch traced here: 170 us
  local copies, waits for them, and re-layouts  40.5 us (24%)
  waiting for transfers between devices  31.5 us (18%)
  other arithmetic  31.2 us (18%)
  blocking collectives  28.2 us (16%)
  matrix products  24.2 us (14%)
  starting transfers between devices  13.7 us (8%)
    all_to_all x1, blocking collectives, shards(): lax.all_to_all(gathered, 'ens', split_axis=0, concat_axis=1, tiled=True)  28.2 us
    all_to_all x1, waiting for transfers between devices, shards(): lax.all_to_all(middle, 'ens', split_axis=1, concat_axis=0, tiled=True)  26.6 us
    reduce_sum x2, other arithmetic, layer_norm(): center = values - jnp.mean(values, axis=-1, keepdims=True)  19.3 us
    dot_general x1, matrix products, mix_members(): jnp.einsum('mphd,nphd->hmnp', split[0], split[1], preferred_element_type=...  8.83 us
    dot_general x1, matrix products, mix_members(): jnp.einsum('hmnp,nphd->mphd', weights, split[2], preferred_element_type=j...  8.34 us
    dot_general x1, local copies, waits for them, and re-layouts, mix_members(): jnp.einsum('mphd,nphd->hmnp', split[0], split[1], preferred_element_type=...  6.82 us
    squeeze x1, local copies, waits for them, and re-layouts, mix_members(): split[1]  6.79 us
    squeeze x1, local copies, waits for them, and re-layouts, mix_members(): split[0]  6.77 us
  transfers between devices with their start and end apart: 5, of which 4 were waited for; matrix products, arithmetic and copies ran while one was open for 1% of the time, Pallas kernels for 0%

commit v1 on v0

--- a/solution.py
+++ b/solution.py
@@ -5,6 +5,22 @@
 
 HEADS = 4
 KERNEL = 7
+
+
+def pairwise_exchange(x, axis, split, join):
+    ways, here = (lax.axis_size(axis), lax.axis_index(axis))
+    width = x.shape[split] // ways
+    dims = list(x.shape)
+    dims[split] = width
+    height = dims[join]
+    dims[join] = height * ways
+    full = jnp.zeros(dims, x.dtype)
+    for mask in range(ways):
+        part = lax.dynamic_slice_in_dim(x, (here ^ mask) * width, width, axis=split)
+        if mask:
+            part = lax.ppermute(part, axis, [(d, d ^ mask) for d in range(ways)])
+        full = lax.dynamic_update_slice_in_dim(full, part, (here ^ mask) * height, axis=join)
+    return full
 
 
 def extended(array, sides, width):
@@ -73,7 +89,7 @@
     middle = (fields.astype(jnp.float32) + layer_scale.astype(jnp.float32) * branch).astype(
         jnp.bfloat16
     )
-    block = lax.all_to_all(middle, "ens", split_axis=1, concat_axis=0, tiled=True)
+    block = pairwise_exchange(middle, "ens", 1, 0)
     count, block_rows, block_cols, block_width = block.shape
     flat_rows = block.reshape(count, block_rows * block_cols, block_width)
     mixed = mix_members(flat_rows, attn_gain, qkv_weight)

time: 171 us -> 186 us (1.088)
  other arithmetic: 31.2 us -> 51 us
  waiting for transfers between devices: 31.5 us -> 18.9 us
  blocking collectives: 28.2 us -> 33.9 us
  local copies, waits for them, and re-layouts: 40.5 us -> 44.4 us
    all_to_all x1 -> x0, waiting for transfers between devices: 26.6 us -> none  [shards(): lax.all_to_all(middle, 'ens', split_axis=1, concat_axis=0, tiled=True)]
    reduce_sum x2, other arithmetic: 19.3 us -> 41.3 us  [layer_norm(): center = values - jnp.mean(values, axis=-1, keepdims=True)]
    ppermute x0 -> x3, waiting for transfers between devices: none -> 18.7 us  [pairwise_exchange(): part = lax.ppermute(part, axis, [(d, d ^ mask) for d in range(ways)])]
    all_to_all x1, blocking collectives: 28.2 us -> 33.9 us  [shards(): lax.all_to_all(gathered, 'ens', split_axis=0, concat_axis=1, tiled=True)]
    ppermute x0 -> x3, starting transfers between devices: none -> 5.32 us  [pairwise_exchange(): part = lax.ppermute(part, axis, [(d, d ^ mask) for d in range(ways)])]
    all_to_all x1 -> x0, starting transfers between devices: 5.01 us -> none  [shards(): lax.all_to_all(middle, 'ens', split_axis=1, concat_axis=0, tiled=True)]
    ppermute x2, waiting for transfers between devices: 4.79 us -> 0.01 us  [extended(): after = lax.ppermute(first, axis, down)]
    convert_element_type x1, other arithmetic: 2.88 us -> 0.33 us  [shards(): (fields.astype(jnp.float32) + layer_scale.astype(jnp.float32) * branch).a...]
  transfers between devices with their start and end apart: 5 -> 7, of which waited for: 4 -> 3; matrix products, arithmetic and copies ran while one was open for 1% -> 4% of each run, Pallas kernels for 0% -> 0%
where the time goes in v1:
time: 186 us
  other arithmetic  51 us (27%)
  local copies, waits for them, and re-layouts  44.4 us (24%)
  blocking collectives  33.9 us (18%)
  matrix products  23 us (12%)
  waiting for transfers between devices  18.9 us (10%)
  starting transfers between devices  14.1 us (8%)
    reduce_sum x2, other arithmetic, layer_norm(): center = values - jnp.mean(values, axis=-1, keepdims=True)  41.3 us
    all_to_all x1, blocking collectives, shards(): lax.all_to_all(gathered, 'ens', split_axis=0, concat_axis=1, tiled=True)  33.9 us
    ppermute x3, waiting for transfers between devices, pairwise_exchange(): part = lax.ppermute(part, axis, [(d, d ^ mask) for d in range(ways)])  18.7 us
    dot_general x1, matrix products, mix_members(): jnp.einsum('mphd,nphd->hmnp', split[0], split[1], preferred_element_type=...  8.83 us
    dot_general x1, matrix products, mix_members(): jnp.einsum('hmnp,nphd->mphd', weights, split[2], preferred_element_type=j...  8.35 us
    dot_general x1, local copies, waits for them, and re-layouts, mix_members(): jnp.einsum('mphd,nphd->hmnp', split[0], split[1], preferred_element_type=...  6.82 us
    squeeze x1, local copies, waits for them, and re-layouts, mix_members(): split[1]  6.77 us
    ppermute x2, starting transfers between devices, extended(): before = lax.ppermute(last, axis, up)  6.2 us
  transfers between devices with their start and end apart: 7, of which 3 were waited for; matrix products, arithmetic and copies ran while one was open for 4% of the time, Pallas kernels for 0%

profile of v1, /device:TPU:0, one launch (start us, length us, event | category | flops | bytes accessed | tf_op | source)
XLA Modules:
  0.0 185.7 jit_solution(18038141689109426230)
XLA Ops:
  0.0 0.0 copy-start
  0.0 1.0 fusion.84
  1.0 1.3 collective-permute-start.1
  2.3 4.9 %collective-permute-start = (bf16[1,3,128,128]{3,2,1,0:T(8,128)(2,1)S(1)}, bf16[1,3,128,128]{3,2,1,0:T(8,128)(2,1)S(1)}, u32[]{:S(2)}, u32[]{:S(2)}) collective-permute-start(bf16[1,3,128,128]{3,2,1,0:T(8,128)(2,1)S(1)} %get-tuple-element.20), channel_id=1, source_target_pairs={{0,2},{1,3},{4,6},{5,7},{8,10},{9,11},{12,14},{13,15},{16,18},{17,... | collective-permute-start | bytes 294920 | tf_op jit(solution)/shard_map/ppermute | solution.py:33
  7.2 0.7 convert_element_type.204
  7.9 0.6 slice_bitcast_fusion.47
  8.5 0.7 slice_bitcast_fusion.48
  9.2 0.1 collective-permute-done
  9.4 0.0 copy-start.1
  9.4 2.2 %constant_dynamic-update-slice_fusion.3 = (bf16[1,35,128,128]{3,2,1,0:T(8,128)(2,1)S(1)}, bf16[1,38,128,128]{3,2,1,0:T(8,128)(2,1)S(1)}, bf16[1,35,128,128]{3,2,1,0:T(8,128)(2,1)S(1)}) fusion(bf16[1,35,128,128]{3,2,1,0:T(8,128)(2,1)S(1)} %get-tuple-element.21, bf16[1,32,128,128]{3,2,1,0:T(8,128)(2,1)} %param.9, ...), kind=kLoop, calls=%fused_computation.150 | loop fusion | bytes 4194304 | tf_op jit(solution)/shard_map/concatenate | solution.py:35
  11.6 0.0 collective-permute-done.1
  11.7 0.0 copy-start.2
  11.7 1.0 copy-done.2
  12.7 0.7 fusion.83
  13.4 1.3 collective-permute-start.2
  14.8 1.3 collective-permute-start.3
  16.1 0.6 slice_bitcast_fusion.46
  16.7 1.1 convert_element_type.252
  17.8 1.2 convert_element_type.202
  19.0 0.0 collective-permute-done.2
  19.0 0.0 collective-permute-done.3
  19.0 0.0 copy-done.1
  19.0 40.9 %fusion.80 = (f32[32,128]{1,0:T(8,128)S(1)}, f32[1,32,128,128]{3,2,1,0:T(8,128)S(1)}) fusion(f32[128]{0:T(128)} %get-tuple-element.26, bf16[1,38,3,128]{3,2,1,0:T(4,128)(2,1)S(1)} %collective-permute-done.3, bf16[1,38,128,128]{3,2,1,0:T(8,128)(2,1)} %copy-done.2, f32[128]{0:T(128)} %get-tuple-element.27, f32[128]{0:T(128)} %get-tuple-element.28, ...), kind=kLoop, calls=%fused_computation.219 | loop fusion | flops 143126528 | bytes 10782208 | tf_op jit(solution)/shard_map/reduce_sum | solution.py:40
  60.0 0.0 copy-start.6
  60.0 1.3 multiply_reduce_fusion
  61.3 0.0 copy-start.7
  61.3 0.0 copy-done.6
  61.4 2.0 %multiply_convert_fusion = bf16[1,32,128,128]{3,2,1,0:T(8,128)(2,1)} fusion(f32[1,32,128,128]{3,2,1,0:T(8,128)S(1)} %get-tuple-element.6, f32[128]{0:T(128)S(1)} %copy-done.6, f32[32,128]{1,0:T(8,128)S(1)} %add_rsqrt_fusion, f32[32,128]{1,0:T(8,128)S(1)} %broadcast_multiply_fusion.1), kind=kLoop, calls=%fused_computation.74 | loop fusion | flops 2097152 | bytes 3179008 | tf_op jit(solution)/shard_map/convert_element_type | solution.py:82
  63.4 0.0 copy-done
  63.4 0.0 copy-done.7
  63.4 4.3 %fusion.25 = f32[4096,128]{1,0:T(8,128)S(1)} fusion(bf16[512,128]{1,0:T(8,128)(2,1)S(1)} %copy-done, bf16[4096,128]{1,0:T(8,128)(2,1)} %bitcast.161, bf16[128,512]{1,0:T(8,128)(2,1)S(1)} %copy-done.7), kind=kOutput, calls=%fused_computation.76 | convolution fusion | flops 1092616192 | bytes 3407872 | tf_op jit(solution)/shard_map/dot_general | solution.py:86
  67.7 0.0 copy-done.5
  67.8 0.3 fusion.18
  68.1 0.0 copy-start.8
  68.1 0.2 broadcast_in_dim.2
  68.3 0.1 constant_dynamic-slice_fusion
  68.4 2.7 %collective-permute-start.4 = (bf16[1,8,128,128]{3,2,1,0:T(8,128)(2,1)S(1)}, bf16[1,8,128,128]{3,2,1,0:T(8,128)(2,1)S(1)}, u32[]{:S(2)}, u32[]{:S(2)}) collective-permute-start(bf16[1,8,128,128]{3,2,1,0:T(8,128)(2,1)S(1)} %get-tuple-element.14), channel_id=1, source_target_pairs={{0,4},{4,0},{8,12},{12,8},{1,5},{5,1},{9,13},{13,9},{2,6},{6,2},{1... | collective-permute-start | bytes 786440 | tf_op jit(solution)/shard_map/ppermute | solution.py:21
  71.2 2.6 %collective-permute-start.5 = (bf16[1,8,128,128]{3,2,1,0:T(8,128)(2,1)S(1)}, bf16[1,8,128,128]{3,2,1,0:T(8,128)(2,1)S(1)}, u32[]{:S(2)}, u32[]{:S(2)}) collective-permute-start(bf16[1,8,128,128]{3,2,1,0:T(8,128)(2,1)S(1)} %get-tuple-element.13), channel_id=1, source_target_pairs={{0,8},{4,12},{8,0},{12,4},{1,9},{5,13},{9,1},{13,5},{2,10},{6,14},... | collective-permute-start | bytes 786440 | tf_op jit(solution)/shard_map/ppermute | solution.py:21
  73.8 0.0 collective-permute-start.6
  73.8 0.0 copy-done.8
  73.8 9.5 %collective-permute-done.4 = bf16[1,8,128,128]{3,2,1,0:T(8,128)(2,1)S(1)} collective-permute-done((bf16[1,8,128,128]{3,2,1,0:T(8,128)(2,1)S(1)}, bf16[1,8,128,128]{3,2,1,0:T(8,128)(2,1)S(1)}, u32[]{:S(2)}, u32[]{:S(2)}) %collective-permute-start.4) | collective-permute-done | bytes 262176 | tf_op jit(solution)/shard_map/ppermute | solution.py:21
  83.4 9.2 %collective-permute-done.5 = bf16[1,8,128,128]{3,2,1,0:T(8,128)(2,1)S(1)} collective-permute-done((bf16[1,8,128,128]{3,2,1,0:T(8,128)(2,1)S(1)}, bf16[1,8,128,128]{3,2,1,0:T(8,128)(2,1)S(1)}, u32[]{:S(2)}, u32[]{:S(2)}) %collective-permute-start.5) | collective-permute-done | bytes 262176 | tf_op jit(solution)/shard_map/ppermute | solution.py:21
  92.6 0.0 collective-permute-done.6
  92.6 0.0 copy-start.3
  92.6 0.3 convert_reduce_fusion
  93.0 1.3 fusion.20
  94.3 1.2 fusion.23
  95.6 0.0 copy-done.3
  95.6 1.0 convert_bitcast_fusion
  96.6 1.3 fusion.82
  97.9 6.8 %copy.23 = bf16[4,1024,4,32]{3,0,1,2:T(4,128)(2,1)} copy(bf16[4,1024,4,32]{1,3,2,0:T(8,128)(2,1)} %bitcast.158) | data formatting | bytes 2097152 | tf_op jit(solution)/shard_map/squeeze | solution.py:54
  104.7 4.7 %copy.24 = bf16[4,1024,4,32]{3,0,1,2:T(4,128)(2,1)} copy(bf16[4,1024,4,32]{1,3,2,0:T(8,128)(2,1)S(1)} %bitcast.157) | data formatting | bytes 2097152 | tf_op jit(solution)/shard_map/squeeze | solution.py:54
  109.4 8.8 %fusion.86 = f32[4,1024,4,4]{3,2,1,0:T(4,128)} fusion(bf16[4,1024,4,32]{3,0,1,2:T(4,128)(2,1)} %copy.23, bf16[4,1024,4,32]{3,0,1,2:T(4,128)(2,1)} %copy.24), kind=kOutput, calls=%fused_computation.224 | convolution fusion | flops 4194304 | bytes 2359296 | tf_op jit(solution)/shard_map/mphd,nphd->hmnp/dot_general | solution.py:53
  118.2 6.8 %copy.25 = f32[4,1024,4,4]{1,2,3,0:T(4,128)S(1)} copy(f32[4,1024,4,4]{3,2,1,0:T(4,128)} %fusion.86) | data formatting | bytes 524288 | tf_op jit(solution)/shard_map/mphd,nphd->hmnp/dot_general | solution.py:53
  125.1 0.4 fusion.85
  125.4 0.1 divide_convert_fusion
  125.5 5.5 %copy.27 = bf16[4,4,4,1024]{2,1,0,3:T(4,128)(2,1)} copy(bf16[4,4,4,1024]{3,2,1,0:T(4,128)(2,1)S(1)} %divide_convert_fusion) | data formatting | bytes 262144 | tf_op jit(solution)/shard_map/convert_element_type | solution.py:58
  131.0 5.4 %copy.26 = bf16[4,1024,4,32]{3,0,2,1:T(4,128)(2,1)} copy(bf16[4,1024,4,32]{1,3,2,0:T(8,128)(2,1)S(1)} %bitcast.156) | data formatting | bytes 2097152 | tf_op jit(solution)/shard_map/squeeze | solution.py:60
  136.4 8.3 %fusion.9 = bf16[4,1024,4,32]{3,0,2,1:T(4,128)(2,1)} fusion(bf16[4,1024,4,32]{3,0,2,1:T(4,128)(2,1)} %copy.26, bf16[4,4,4,1024]{2,1,0,3:T(4,128)(2,1)} %copy.27), kind=kOutput, calls=%fused_computation.51 | convolution fusion | flops 4718592 | bytes 2228224 | tf_op jit(solution)/shard_map/hmnp,nphd->mphd/dot_general | solution.py:59
  144.7 5.5 %copy.28 = bf16[4,1024,4,32]{1,3,2,0:T(8,128)(2,1)S(1)} copy(bf16[4,1024,4,32]{3,0,2,1:T(4,128)(2,1)} %fusion.9) | data formatting | bytes 2097152 | tf_op jit(solution)/shard_map/convert_element_type | solution.py:61
  150.2 0.0 copy-done.4
  150.2 0.5 fusion.24
  150.7 33.9 %all_to_all.12 = bf16[4,8,128,128]{3,2,1,0:T(8,128)(2,1)S(1)} all-to-all(bf16[4,8,128,128]{3,2,1,0:T(8,128)(2,1)S(1)} %bitcast.155), channel_id=1, replica_groups=mesh['group'=2,'ens'=4,'row'=2,'col'=2] {'ens'}, dimensions={0} | all-to-all | bytes 2097152 | tf_op jit(solution)/shard_map/all_to_all | solution.py:100
  184.7 1.0 copy.47
  (13 shorter events, 0.2 us)
Async XLA Ops:
  0.0 63.4 %copy-start = (bf16[512,128]{1,0:T(8,128)(2,1)S(1)}, bf16[512,128]{1,0:T(8,128)(2,1)}, u32[]{:S(2)}) copy-start(bf16[512,128]{1,0:T(8,128)(2,1)} %param.13) | copy-start | bytes 393220
  1.0 10.6 %collective-permute-start.1 = (bf16[1,3,128,128]{3,2,1,0:T(8,128)(2,1)S(1)}, bf16[1,3,128,128]{3,2,1,0:T(8,128)(2,1)S(1)}, u32[]{:S(2)}, u32[]{:S(2)}) collective-permute-start(bf16[1,3,128,128]{3,2,1,0:T(8,128)(2,1)S(1)} %get-tuple-element.19), channel_id=1, source_target_pairs={{2,0},{3,1},{6,4},{7,5},{10,8},{11,9},{14,12},{15,13},{18,16},{19,... | collective-permute-start | bytes 294920 | tf_op jit(solution)/shard_map/ppermute | solution.py:34
  2.3 7.0 %collective-permute-start = (bf16[1,3,128,128]{3,2,1,0:T(8,128)(2,1)S(1)}, bf16[1,3,128,128]{3,2,1,0:T(8,128)(2,1)S(1)}, u32[]{:S(2)}, u32[]{:S(2)}) collective-permute-start(bf16[1,3,128,128]{3,2,1,0:T(8,128)(2,1)S(1)} %get-tuple-element.20), channel_id=1, source_target_pairs={{0,2},{1,3},{4,6},{5,7},{8,10},{9,11},{12,14},{13,15},{16,18},{17,... | collective-permute-start | bytes 294920 | tf_op jit(solution)/shard_map/ppermute | solution.py:33
  9.4 9.6 %copy-start.1 = (bf16[1,32,128,128]{3,2,1,0:T(8,128)(2,1)S(1)}, bf16[1,32,128,128]{3,2,1,0:T(8,128)(2,1)}, u32[]{:S(2)}) copy-start(bf16[1,32,128,128]{3,2,1,0:T(8,128)(2,1)} %param.9) | copy-start | bytes 3145732
  11.7 1.0 copy-start.2
  13.4 5.6 %collective-permute-start.2 = (bf16[1,38,3,128]{3,2,1,0:T(4,128)(2,1)}, bf16[1,38,3,128]{3,2,1,0:T(4,128)(2,1)S(1)}, u32[]{:S(2)}, u32[]{:S(2)}) collective-permute-start(bf16[1,38,3,128]{3,2,1,0:T(4,128)(2,1)} %get-tuple-element.10), channel_id=1, source_target_pairs={{0,1},{2,3},{4,5},{6,7},{8,9},{10,11},{12,13},{14,15},{16,17},{18,... | collective-permute-start | bytes 87560 | tf_op jit(solution)/shard_map/ppermute | solution.py:33
  14.8 4.3 %collective-permute-start.3 = (bf16[1,38,3,128]{3,2,1,0:T(4,128)(2,1)}, bf16[1,38,3,128]{3,2,1,0:T(4,128)(2,1)S(1)}, u32[]{:S(2)}, u32[]{:S(2)}) collective-permute-start(bf16[1,38,3,128]{3,2,1,0:T(4,128)(2,1)} %get-tuple-element.11), channel_id=1, source_target_pairs={{1,0},{3,2},{5,4},{7,6},{9,8},{11,10},{13,12},{15,14},{17,16},{19,... | collective-permute-start | bytes 87560 | tf_op jit(solution)/shard_map/ppermute | solution.py:34
  60.0 1.4 copy-start.6
  61.3 2.1 %copy-start.7 = (bf16[128,512]{1,0:T(8,128)(2,1)S(1)}, bf16[128,512]{1,0:T(8,128)(2,1)}, u32[]{:S(2)}) copy-start(bf16[128,512]{1,0:T(8,128)(2,1)} %param.12) | copy-start | bytes 393220
  63.4 4.3 %copy-start.5 = (f32[128]{0:T(128)S(1)}, f32[128]{0:T(128)}, u32[]{:S(2)}) copy-start(f32[128]{0:T(128)} %convert_element_type.202) | copy-start | bytes 1540
  68.1 5.7 %copy-start.8 = (bf16[128]{0:T(256)(128)(2,1)S(1)}, bf16[128]{0:T(256)(128)(2,1)}, u32[]{:S(2)}) copy-start(bf16[128]{0:T(256)(128)(2,1)} %param.15) | copy-start | bytes 772
  68.4 14.9 %collective-permute-start.4 = (bf16[1,8,128,128]{3,2,1,0:T(8,128)(2,1)S(1)}, bf16[1,8,128,128]{3,2,1,0:T(8,128)(2,1)S(1)}, u32[]{:S(2)}, u32[]{:S(2)}) collective-permute-start(bf16[1,8,128,128]{3,2,1,0:T(8,128)(2,1)S(1)} %get-tuple-element.14), channel_id=1, source_target_pairs={{0,4},{4,0},{8,12},{12,8},{1,5},{5,1},{9,13},{13,9},{2,6},{6,2},{1... | collective-permute-start | bytes 786440 | tf_op jit(solution)/shard_map/ppermute | solution.py:21
  71.2 21.4 %collective-permute-start.5 = (bf16[1,8,128,128]{3,2,1,0:T(8,128)(2,1)S(1)}, bf16[1,8,128,128]{3,2,1,0:T(8,128)(2,1)S(1)}, u32[]{:S(2)}, u32[]{:S(2)}) collective-permute-start(bf16[1,8,128,128]{3,2,1,0:T(8,128)(2,1)S(1)} %get-tuple-element.13), channel_id=1, source_target_pairs={{0,8},{4,12},{8,0},{12,4},{1,9},{5,13},{9,1},{13,5},{2,10},{6,14},... | collective-permute-start | bytes 786440 | tf_op jit(solution)/shard_map/ppermute | solution.py:21
  73.8 18.8 %collective-permute-start.6 = (bf16[1,8,128,128]{3,2,1,0:T(8,128)(2,1)S(1)}, bf16[1,8,128,128]{3,2,1,0:T(8,128)(2,1)S(1)}, u32[]{:S(2)}, u32[]{:S(2)}) collective-permute-start(bf16[1,8,128,128]{3,2,1,0:T(8,128)(2,1)S(1)} %get-tuple-element.12), channel_id=1, source_target_pairs={{0,12},{4,8},{8,4},{12,0},{1,13},{5,9},{9,5},{13,1},{2,14},{6,10},... | collective-permute-start | bytes 786440 | tf_op jit(solution)/shard_map/ppermute | solution.py:21
  92.6 3.0 %copy-start.3 = (bf16[3,128,128]{2,1,0:T(8,128)(2,1)S(1)}, bf16[3,128,128]{2,1,0:T(8,128)(2,1)}, u32[]{:S(2)}) copy-start(bf16[3,128,128]{2,1,0:T(8,128)(2,1)} %param.16) | copy-start | bytes 294916
  144.7 5.5 %copy-start.4 = (bf16[128,128]{1,0:T(8,128)(2,1)S(1)}, bf16[128,128]{1,0:T(8,128)(2,1)}, u32[]{:S(2)}) copy-start(bf16[128,128]{1,0:T(8,128)(2,1)} %param.17) | copy-start | bytes 98308
